TPU v7x, 32 devices: a whole 2x2x4 slice. The times are simulated.
32 devices in a mesh: seq: 4 (over x, core), dp: 8 (over z, y).
Axes of the slice: x: 2, y: 2, z: 4, core: 2. Of those that a mesh axis runs over, the one named last changes fastest.
Arguments:
- tokens: bfloat16 [8, 512, 768], P('dp', 'seq'), may hold values from -6 to 6
- memory: bfloat16 [8, 1024, 768], P('dp', 'seq'), may hold values from -6 to 6
- target_segments: int32 [8, 512], P('dp'), may hold values from 0 to 254, as said below
- memory_segments: int32 [8, 1024], P('dp'), may hold values from 0 to 254, as said below
- pad_counts: int32 [8, 2], P('dp'), may hold values from 0 to 252, as said below
- out_grad: bfloat16 [8, 512, 768], P('dp', 'seq'), may hold values from -6 to 6
- self_query: bfloat16 [768, 768], replicated, may hold values from -0.21875 to 0.21875
- self_key: bfloat16 [768, 768], replicated, may hold values from -0.21875 to 0.21875
- self_value: bfloat16 [768, 768], replicated, may hold values from -0.21875 to 0.21875
- self_out: bfloat16 [768, 768], replicated, may hold values from -0.875 to 0.875
- cross_query: bfloat16 [768, 768], replicated, may hold values from -0.21875 to 0.21875
- cross_key: bfloat16 [768, 768], replicated, may hold values from -0.21875 to 0.21875
- cross_value: bfloat16 [768, 768], replicated, may hold values from -0.21875 to 0.21875
- cross_out: bfloat16 [768, 768], replicated, may hold values from -0.875 to 0.875
- feed_in: bfloat16 [768, 3072], replicated, may hold values from -0.21875 to 0.21875
- feed_out: bfloat16 [3072, 768], replicated, may hold values from -0.109375 to 0.109375
- gain_attend: bfloat16 [768], replicated, may hold values from 0.099609375 to 1.8984375
- shift_attend: bfloat16 [768], replicated, may hold values from -3 to 3
- gain_cross: bfloat16 [768], replicated, may hold values from 0.099609375 to 1.8984375
- shift_cross: bfloat16 [768], replicated, may hold values from -3 to 3
- gain_feed: bfloat16 [768], replicated, may hold values from 0.099609375 to 1.8984375
- shift_feed: bfloat16 [768], replicated, may hold values from -3 to 3
Outputs:
- layer_out: float32 [8, 512, 768], P('dp', 'seq')
- tokens_grad: float32 [8, 512, 768], P('dp', 'seq')
- memory_grad: float32 [8, 1024, 768], P('dp', 'seq')
- grad_self_query: float32 [768, 768], P('dp')
- grad_self_key: float32 [768, 768], P('dp')
- grad_self_value: float32 [768, 768], P('dp')
- grad_self_out: float32 [768, 768], P('dp')
- grad_cross_query: float32 [768, 768], P('dp')
- grad_cross_key: float32 [768, 768], P('dp')
- grad_cross_value: float32 [768, 768], P('dp')
- grad_cross_out: float32 [768, 768], P('dp')
- grad_feed_in: float32 [768, 3072], P('dp')
- grad_feed_out: float32 [3072, 768], P('dp')
- grad_gain_attend: float32 [768], P('dp')
- grad_shift_attend: float32 [768], P('dp')
- grad_gain_cross: float32 [768], P('dp')
- grad_shift_cross: float32 [768], P('dp')
- grad_gain_feed: float32 [768], P('dp')
- grad_shift_feed: float32 [768], P('dp')
Inputs may be any that keep to these rules, and one draw needn't show every extreme that they name: `target_segments`: in each row ids start at 0, never fall, and rise by at most one from one position to the next; the padded tail of a row continues its last document. `memory_segments`: in each row ids start at 0, never fall and rise by at most one from one position to the next; the unpadded memory of a row holds each id of the row's targets, every one of them, and no other. `pad_counts`: column 0 counts padded target positions, column 1 padded memory positions; the memory of a row's last document is never wholly padded; some row has no padding.
All inputs are finite; a program needn't handle non-finite values.
Results may differ from a plain program's by a relative error of at most 0.018.
Values may be sent and summed in bfloat16 or wider, within the bound.
A program may use at most 192 MiB of HBM per device.

v0:
```python
import functools

import jax
import jax.numpy as jnp
from jax import lax
from jax.experimental import pallas as pl
from jax.experimental.pallas import tpu as pltpu
from jax.sharding import PartitionSpec as P

HEAD_DIM = 64
EPSILON = 1e-05
NEGATIVE = -1e30
F32 = jnp.float32
BF16 = jnp.bfloat16
MESH = pl.DeviceIdType.MESH
WINDOW = 256
CHUNKS = 2


def mm(left, right):
    return jnp.dot(left, right, preferred_element_type=F32)


def mm_t(left, right):
    return lax.dot_general(left, right, (((1,), (1,)), ((), ())), preferred_element_type=F32)


def t_mm(left, right):
    return lax.dot_general(left, right, (((0,), (0,)), ((), ())), preferred_element_type=F32)


def normalize(values):
    centered = values - jnp.mean(values, axis=-1, keepdims=True)
    rate = lax.rsqrt(jnp.mean(centered * centered, axis=-1, keepdims=True) + EPSILON)
    return centered * rate, rate


def norm_back(grad, gain, normed, rate):
    scaled = grad * gain
    inner = jnp.mean(scaled * normed, axis=-1, keepdims=True)
    return rate * (scaled - jnp.mean(scaled, axis=-1, keepdims=True) - normed * inner)


class Names:
    def __init__(self, names, refs):
        self.__dict__.update(zip(names, refs))


INPUTS = ["tokens", "memory", "out_grad", "target_ids", "memory_ids", "pads"]
INPUTS += ["w_sq", "w_sk", "w_sv", "w_so", "w_cq", "w_ck", "w_cv", "w_co", "w_fi", "w_fo"]
INPUTS += ["gain_a", "shift_a", "gain_c", "shift_c", "gain_f", "shift_f"]
OUTPUTS = ["o_layer", "o_tokens", "o_memory", "o_stats"]
SEMAPHORES = ["load_sem", "send_sem", "recv_sem"]
GROUPS = ["g_fo", "g_fi", "g_cross", "g_self"]
ALONG, ACROSS, MIXED, TURNED = (1, 2, 0), (0, 1, 2), (1, 0, 2), (0, 2, 1)
ORDERS = (ACROSS, ALONG, ALONG, ACROSS, ACROSS, ACROSS, ACROSS, ACROSS)
STRAIGHT = 6
CUTS = (2, 1, 1, 6)
(
    OWN_FI, TOKENS_NEAR, TOKENS_MIDDLE, TOKENS_FAR, MEMORY_NEAR, MEMORY_MIDDLE, MEMORY_FAR, TOKENS_RELAY, MEMORY_RELAY,
    COTANGENT_SEND, COTANGENT_RELAY, LAYER_SEND, LAYER_SECOND, LAYER_OUT, MEMORY_TERMS,
    MEMORY_SECOND, MEMORY_OUT, TOKEN_TERMS, TOKEN_SECOND, TOKEN_OUT, GRAD_FO, GRAD_FI, GRAD_CK,
    GRAD_CV, GRAD_CO, GRAD_CQ, GRAD_SO, GRAD_SQ, GRAD_SK, GRAD_SV, NORMS_SEND,
) = range(31)
(
    SELF, ROWS, CROSS, FEED_UP, FEED_BACK, LAYER, CROSS_GRAD, CROSS_BACK, SELF_GRAD, SELF_BACK,
    CROSS_RELAY, ROWS_RELAY, TOTAL_SECOND, TOTAL_THIRD, NORMS_STEP,
) = range(100, 115)
OUT, W_SO, W_CO, W_FO = range(4)
SCHEDULE = [
    OWN_FI, TOKENS_NEAR, MEMORY_NEAR, TOKENS_RELAY, TOKENS_MIDDLE, TOKENS_FAR, (SELF, 1), (SELF, 0),
    (ROWS, 1), COTANGENT_SEND, (ROWS, 0), MEMORY_RELAY, MEMORY_MIDDLE, MEMORY_FAR, (CROSS, 0),
    (CROSS, 1), COTANGENT_RELAY, (CROSS_RELAY, 0), (FEED_UP, 0), (CROSS_RELAY, 1), (FEED_BACK, 0),
    (FEED_UP, 1), (TOTAL_SECOND, 0), GRAD_FO, (LAYER, 1), (1, 0, 0), (0, 0, 0), (FEED_BACK, 1),
    GRAD_FI, (3, 0, 0), (2, 0, 0), (TOTAL_SECOND, 1), (LAYER, 0), LAYER_SEND, (0, 1, 0), (1, 1, 0),
    (TOTAL_THIRD, 0), LAYER_SECOND, (1, 0, 1), (0, 0, 1), (CROSS_GRAD, 0), (CROSS_BACK, 0),
    (TOTAL_THIRD, 1), (CROSS_GRAD, 1), GRAD_CO, (CROSS_BACK, 1), GRAD_CK, (4, 0, 0), (ROWS_RELAY, 0),
    (1, 1, 1), GRAD_CQ, LAYER_OUT, (1, 0, 2), (3, 0, 1), (0, 1, 1), GRAD_CV, (0, 0, 2), (5, 0, 0),
    MEMORY_TERMS, (ROWS_RELAY, 1), (2, 0, 1), (SELF_GRAD, 0), (1, 1, 2), MEMORY_SECOND, (SELF_GRAD, 1),
    GRAD_SO, (7, 0, 0), (3, 0, 2), (4, 0, 1), (SELF_BACK, 1), (SELF_BACK, 0), GRAD_SK, GRAD_SV,
    (7, 4, 0), (7, 1, 0), (7, 2, 0), TOKEN_TERMS, (7, 3, 0), (0, 1, 2), (5, 0, 1), (1, 0, 3),
    NORMS_SEND, GRAD_SQ, TOKEN_SECOND, (NORMS_STEP, 0), (6, 0, 0), (7, 0, 1), (2, 0, 2), (4, 0, 2),
    MEMORY_OUT, (7, 5, 0), (7, 4, 1), (0, 0, 3), (6, 1, 0), (6, 2, 0), (6, 3, 0), (6, 4, 0), (6, 5, 0),
    (3, 0, 3), (1, 0, 4), (7, 1, 1), (1, 1, 3), (7, 2, 1), (1, 0, 5), (0, 1, 3), (7, 3, 1), (5, 0, 2),
    (7, 0, 2), (6, 0, 1), TOKEN_OUT, (NORMS_STEP, 1), (2, 0, 3), (4, 0, 3), (7, 4, 2), (0, 0, 4),
    (7, 1, 2), (7, 5, 1), (7, 2, 2), (0, 0, 5), (7, 3, 2), (6, 1, 1), (3, 0, 4), (1, 1, 4), (6, 2, 1),
    (3, 0, 5), (0, 1, 4), (5, 0, 3), (6, 0, 2), (6, 3, 1), (1, 1, 5), (7, 0, 3), (0, 1, 5), (7, 4, 3),
    (6, 4, 1), (7, 5, 2), (7, 1, 3), (2, 0, 4), (7, 2, 3), (6, 5, 1), (6, 1, 2), (7, 3, 3),
    (NORMS_STEP, 2), (2, 0, 5), (6, 2, 2), (4, 0, 4), (6, 3, 2), (6, 0, 3), (6, 4, 2), (4, 0, 5),
    (5, 0, 4), (7, 5, 3), (7, 0, 5), (6, 5, 2), (7, 4, 5), (5, 0, 5), (6, 1, 3), (NORMS_STEP, 3),
    (7, 1, 5), (7, 2, 5), (6, 2, 3), (7, 3, 5), (6, 3, 3), (6, 0, 5), (6, 4, 3), (7, 5, 5), (6, 5, 3),
    (6, 1, 5), (6, 2, 5), (NORMS_STEP, 4), (6, 3, 5), (6, 4, 5), (6, 5, 5),
]


def row_kernel(scratch_names, seq, direct, *refs):
    r = Names(INPUTS + OUTPUTS + (["o_sums"] if direct else GROUPS) + scratch_names, refs)
    me = lax.axis_index("seq")
    core = lax.rem(me, 2)
    chip = me // 2
    peer_c = me + 1 - 2 * core
    peer_x = lax.rem(me + 2, 4)
    span = r.tokens.shape[0]
    full, width = r.row.shape
    src_span = r.memory.shape[0]
    src_full = src_span * seq
    part = width // seq
    count = part // HEAD_DIM
    size = full // CHUNKS
    odd = chip
    half_width = 2 * part
    core_window = pl.ds(pl.multiple_of(core * half_width, 128), half_width)
    window = pl.ds(pl.multiple_of(core * half_width + chip * 128, 128), WINDOW)
    own_window = pl.ds(pl.multiple_of(chip * 128, 128), WINDOW)
    own_rows = pl.ds(pl.multiple_of((2 * core + chip) * part, 64), part)
    own_head, other_head = chip * count, (1 - chip) * count
    own_span = pl.ds(pl.multiple_of(me * span, span), span)

    def pick(value):
        return jnp.where(odd == 1, value[:, 64 : 64 + part], value[:, :part])

    def place(value):
        empty = jnp.zeros((value.shape[0], WINDOW - part), value.dtype)
        return jnp.where(
            odd == 1,
            jnp.concatenate([empty, value], 1),
            jnp.concatenate([value, empty], 1),
        )

    loads = []

    def load(src, dst):
        copy = pltpu.make_async_copy(src, dst, r.load_sem.at[len(loads)])
        copy.start()
        loads.append(copy)
        return copy

    stores = []

    def store(src, dst):
        stores.append(load(src, dst))

    def ready(*copies):
        for copy in copies:
            copy.wait()

    place_dp = lax.axis_index("dp")
    peers = [{"seq": peer_c}, {"seq": peer_x}]
    to_core, to_chip = peers
    to_far = {"seq": lax.rem(peer_c + 2, 4)}
    bits, peers_dp = [], []
    if direct:
        for level in range(3):
            bit = lax.rem(place_dp // 2**level, 2)
            bits.append(bit)
            peers_dp.append({"dp": place_dp + 2**level * (1 - 2 * bit)})
    barrier = pltpu.get_barrier_semaphore()
    others = peers + peers_dp + ([to_far] if direct else [])
    for peer in others:
        pl.semaphore_signal(barrier, inc=1, device_id=peer, device_id_type=MESH)

    own_source = pl.ds(pl.multiple_of(me * src_span, src_span), src_span)
    get_tok = load(r.tokens, r.row.at[own_span])
    get_sq = load(r.w_sq.at[:, core_window], r.win_sq)
    get_sk = load(r.w_sk.at[:, core_window], r.win_sk)
    get_sv = load(r.w_sv.at[:, core_window], r.win_sv)
    get_mem = load(r.memory, r.mem.at[own_source])
    get_ck = load(r.w_ck.at[:, window], r.win_ck)
    get_cv = load(r.w_cv.at[:, window], r.win_cv)
    get_fi, get_fo = [], []
    if direct:
        blocks, share = r.g_fo.shape[0] * 4, r.g_fo.shape[3]
        unit = share

        def wide_fi(b):
            spot = pl.ds(pl.multiple_of(b % 4 * WINDOW, WINDOW), WINDOW)
            return r.cross_weights.at[pl.ds(pl.multiple_of(b // 4 * width, width), width), spot]

        for b in range(blocks):
            start = pl.multiple_of(b * (seq * unit) + chip * 128, 128)
            get_fi.append(load(r.w_fi.at[:, pl.ds(start, WINDOW)], wide_fi(b)))
        for b in range(blocks):
            start = pl.multiple_of((b * seq + me) * unit, 16)
            get_fo.append(load(r.w_fo.at[pl.ds(start, unit)], r.own_fo.at[pl.ds(b * unit, unit)]))
    else:
        get_fi = [load(r.w_fi, r.own_fi)]
        get_fo = [load(r.w_fo, r.own_fo)]
    get_so = load(r.w_so, r.all_so)
    get_cq = load(r.w_cq, r.all_cq)
    get_co = load(r.w_co, r.all_co)
    get_og = load(r.out_grad, r.grad_out.at[own_span])

    def column(ids):
        return jnp.broadcast_to(ids.astype(F32), (128, ids.shape[1])).T[:, :1]

    target_ids = r.target_ids[...]
    memory_ids = r.memory_ids[...]
    self_code = jnp.where(
        lax.broadcasted_iota(jnp.int32, (1, full), 1) < full - r.pads[0, 0], target_ids, -1
    ).astype(F32)
    cross_code = jnp.where(
        lax.broadcasted_iota(jnp.int32, (1, src_full), 1) < src_full - r.pads[0, 1], memory_ids, -1
    ).astype(F32)
    target_col = column(target_ids)
    r.target_col[...] = target_col

    def bias_rows(at, carry):
        rows = pl.ds(pl.multiple_of(at * span, span), span)
        i_pos = lax.broadcasted_iota(jnp.int32, (span, full), 0) + at * span
        j_pos = lax.broadcasted_iota(jnp.int32, (span, full), 1)
        same = r.target_col[rows, :] == self_code
        r.self_bias[rows, :] = jnp.where((same & (j_pos <= i_pos)) | (i_pos == j_pos), 0.0, NEGATIVE)
        return carry

    lax.fori_loop(0, seq, bias_rows, 0)
    r.cross_code[...] = cross_code

    def self_masked(scores, rows, reach):
        return scores + r.self_bias[rows, :reach]

    def cross_masked(scores, rows, reach):
        return jnp.where(r.target_col[rows, :] == r.cross_code[:, :reach], scores, NEGATIVE)

    gain_a, shift_a, gain_c, shift_c, gain_f, shift_f = (
        getattr(r, name)[...].astype(F32).reshape(1, width) for name in INPUTS[-6:]
    )
    pl.semaphore_wait(barrier, len(others))

    sent, busy = [], []

    def send(src, dst, peer):
        at = len(sent)
        copy = pltpu.make_async_remote_copy(
            src_ref=src,
            dst_ref=dst,
            send_sem=r.send_sem.at[at],
            recv_sem=r.recv_sem.at[at],
            device_id=peer,
            device_id_type=MESH,
        )
        copy.start()
        sent.append(copy)
        busy.append(copy)
        return copy

    def finish(copies):
        for copy in copies:
            copy.wait_send()
            busy[:] = [other for other in busy if other is not copy]

    class Gather:
        def __init__(self, src, spot):
            self.spot = spot
            self.x = send(src, spot(me), to_chip)
            self.c = send(src, spot(me), to_core)

        def near(self):
            self.c.wait_recv()

        def relay(self):
            self.x.wait_recv()
            self.second = send(self.spot(peer_x), self.spot(peer_x), to_core)

        def far(self):
            self.second.wait_recv()

        def wait(self):
            self.near()
            self.far()

    def rows_at(ref, length):
        return lambda who: ref.at[pl.ds(pl.multiple_of(who * length, length), length)]

    tok = Gather(r.tokens, rows_at(r.row, span))
    mem = Gather(r.memory, rows_at(r.mem, src_span))
    tasks = {}

    class kept:
        to_self, to_cross, to_rows, total, slope, ended = {}, {}, {}, {}, {}, {}
        seen = set()

    def once(what):
        first = what not in kept.seen
        kept.seen.add(what)
        return first

    def task(name):
        def keep(function):
            tasks[name] = function

        return keep

    @task(OWN_FI)
    def _():
        if not direct:
            return
        from_row = lax.broadcasted_iota(jnp.int32, (WINDOW, WINDOW), 0)
        to_col = lax.broadcasted_iota(jnp.int32, (WINDOW, WINDOW), 1)
        skip = me * unit - chip * 128
        ready(*get_fi)
        def tile(t, carry):
            total = None
            for near in range(4):
                b = 2 * t + near
                at = to_col + (t * WINDOW - b * unit)
                chosen = (from_row == at + skip) & (at >= 0) & (at < unit)
                term = mm(wide_fi(b)[...], jnp.where(chosen, 1.0, 0.0).astype(BF16))
                total = term if total is None else total + term
            r.own_fi[:, pl.ds(pl.multiple_of(t * WINDOW, WINDOW), WINDOW)] = total.astype(BF16)
            return carry

        lax.fori_loop(0, blocks * unit // WINDOW, tile, 0)

    def to_heads(value, ref, rows):
        ones = jnp.ones((value.shape[0], HEAD_DIM), ref.dtype)
        for h in range(value.shape[1] // HEAD_DIM):
            head = value[:, h * HEAD_DIM : (h + 1) * HEAD_DIM].astype(ref.dtype)
            ref[h, rows, :] = head if ref.shape[2] == HEAD_DIM else jnp.concatenate([head, ones], 1)

    def part_of(who, length):
        return pl.ds(pl.multiple_of(who * length, length), length)

    def project_tokens(rows):
        row = r.row[rows, :].astype(F32)
        normed, _ = normalize(row)
        r.n_attend[rows, :] = normed.astype(BF16)
        hidden = (normed * gain_a + shift_a).astype(BF16)
        r.h_attend[rows, :] = hidden
        r.after[rows, :] = row
        to_heads(mm(hidden, r.win_sq[...]) * HEAD_DIM**-0.5, r.q, rows)
        to_heads(mm(hidden, r.win_sk[...]), r.k, rows)
        to_heads(mm(hidden, r.win_sv[...]), r.v, rows)

    def project_memory(rows):
        source = r.mem[rows, :]
        to_heads(pick(mm(source, r.win_ck[...])), r.mk, rows)
        to_heads(pick(mm(source, r.win_cv[...])), r.mv, rows)

    @task(TOKENS_NEAR)
    def _():
        ready(get_tok, get_sq, get_sk, get_sv)
        tok.near()
        project_tokens(part_of(chip, full // 2))

    @task(MEMORY_NEAR)
    def _():
        ready(get_mem, get_ck, get_cv)
        mem.near()
        project_memory(part_of(chip, src_full // 2))

    tasks[TOKENS_RELAY] = tok.relay

    @task(TOKENS_MIDDLE)
    def _():
        project_tokens(part_of(peer_x, span))

    @task(TOKENS_FAR)
    def _():
        tok.far()
        project_tokens(part_of(3 - me, span))

    tasks[MEMORY_RELAY] = mem.relay

    @task(MEMORY_MIDDLE)
    def _():
        project_memory(part_of(peer_x, src_span))

    @task(MEMORY_FAR)
    def _():
        mem.far()
        project_memory(part_of(3 - me, src_span))

    def attend(q, k, v, masked, weights, mixed, rows, reach, base=0):
        def one(h):
            scores = masked(mm_t(q[base + h, rows, :], k[base + h, :reach, :]), rows, reach)
            highest = jnp.max(scores, axis=-1, keepdims=True)
            low = jnp.exp(scores - highest).astype(BF16)
            product = mm(low, v[base + h, :reach, :])
            over = 1.0 / product[:, HEAD_DIM : HEAD_DIM + 1]
            head = product[:, :HEAD_DIM] * over
            if weights is not None:
                weights[h * full + rows.start : h * full + rows.stop, :reach] = low
                mixed[h, rows, HEAD_DIM : HEAD_DIM + 1] = over
                mixed[h, rows, :HEAD_DIM] = head
            return head.astype(BF16)

        return [one(h) for h in range(count)]

    def attend_back(q, k, v, grad, weights, mixed, dk, dv, rows, reach, first, base=0):
        def one(h):
            scaled = grad[h, rows, :].astype(F32) * mixed[h, rows, HEAD_DIM : HEAD_DIM + 1]
            inner = jnp.sum(scaled * mixed[h, rows, :HEAD_DIM], axis=-1, keepdims=True)
            low = scaled.astype(BF16)
            exponent = weights[h * full + rows.start : h * full + rows.stop, :reach]
            grad_weights = mm_t(low, v[base + h, :reach, :HEAD_DIM])
            grad_scores = (exponent.astype(F32) * (grad_weights - inner)).astype(BF16)
            grad_q = mm(grad_scores, k[base + h, :reach, :]) * HEAD_DIM**-0.5
            more_k = mm(q[base + h, rows, :].T, grad_scores)
            more_v = mm(low.T, exponent)
            if first:
                dk[h, :, :reach] = more_k
                dv[h, :, :reach] = more_v
            else:
                dk[h, :, :reach] += more_k
                dv[h, :, :reach] += more_v
            return grad_q.astype(BF16)

        return [one(h) for h in range(count)]

    chunks = [slice(c * size, (c + 1) * size) for c in range(CHUNKS)]
    half = size // 2

    def gather_columns(buffer, c, heads):
        buffer[c, me, :size, :] = jnp.concatenate(heads[:2], axis=1)
        buffer[c, me, size:, :] = jnp.concatenate([heads[2][:half], heads[2][half:]], axis=1)
        return Gather(buffer.at[c, me], lambda who: buffer.at[c, who])

    def joined(buffer, c):
        pieces = []
        for s in (0, 2, 1, 3):
            last = buffer[c, s, size:, :]
            pieces.append(buffer[c, s, :size, :])
            pieces.append(jnp.concatenate([last[:, :HEAD_DIM], last[:, HEAD_DIM:]], axis=0))
        return jnp.concatenate(pieces, axis=1)

    def self_chunk(c, rows):
        ours, theirs = (
            jnp.concatenate(attend(r.q, r.k, r.v, self_masked, weights, mix, rows, rows.stop, base), 1)
            for weights, mix, base in (
                (r.self_weights, r.self_mix, own_head),
                (None, None, other_head),
            )
        )
        first, second = jnp.where(chip == 0, ours, theirs), jnp.where(chip == 0, theirs, ours)
        spot = r.self_mixed.at[rows, core_window]
        spot[...] = jnp.concatenate([first, second], axis=1)
        kept.to_self[c] = send(spot, spot, to_core)

    @task(COTANGENT_SEND)
    def _():
        kept.out = Gather(r.out_grad, rows_at(r.grad_out, span))

    @task(COTANGENT_RELAY)
    def _():
        kept.out.relay()

    def out_wait():
        if once(OUT):
            ready(get_og)
            kept.out.wait()

    def cross_rows(c, rows):
        if once(W_SO):
            ready(get_so, get_cq)
        kept.to_self[c].wait_recv()
        after = r.after[rows, :] + mm(r.self_mixed[rows, :], r.all_so[...])
        r.after[rows, :] = after
        normed, rate = normalize(after)
        r.n_cross[rows, :] = normed.astype(BF16)
        r.r_cross[rows, :] = rate
        hidden = (normed * gain_c + shift_c).astype(BF16)
        r.h_cross[rows, :] = hidden
        to_heads(pick(mm(hidden, r.all_cq[:, window])) * HEAD_DIM**-0.5, r.cq, rows)

    def cross_chunk(c, rows):
        heads = attend(
            r.cq, r.mk, r.mv, cross_masked, r.cross_weights, r.cross_mix, rows, src_full
        )
        kept.to_cross[c] = gather_columns(r.cross_parts, c, heads)

    stats = [None] * 6

    def add(name, value):
        value = jnp.sum(value, axis=0, keepdims=True)
        stats[name] = value if stats[name] is None else stats[name] + value

    class Total:
        def __init__(self, c, value):
            self.c = c
            self.keep = part_of(core, half)
            r.sum_send[c] = value.astype(BF16)
            self.step = send(r.sum_send.at[c, part_of(1 - core, half)], r.sum_core.at[c], to_core)

        def second(self):
            self.step.wait_recv()
            r.sum_mid[self.c] = r.sum_send[self.c, self.keep, :] + r.sum_core[self.c]
            self.step = send(r.sum_mid.at[self.c], r.sum_chip.at[self.c], to_chip)

        def third(self):
            self.step.wait_recv()
            r.sum_full[self.c, self.keep, :] = r.sum_mid[self.c] + r.sum_chip[self.c]
            spot = r.sum_full.at[self.c, self.keep]
            self.step = send(spot, spot, to_core)

        def wait(self):
            self.step.wait_recv()
            return r.sum_full[self.c].astype(F32)

    class Scatter:
        def __init__(self, mail, core_in, chip_in):
            self.mail, self.core_in, self.chip_in = mail, core_in, chip_in
            self.steps = [
                send(mail.at[2 * spot + 1 - core], core_in.at[spot], to_core) for spot in range(2)
            ]

        def second(self):
            for step in self.steps:
                step.wait_recv()
            away = 1 - chip
            self.mail[2 * away + core] += self.core_in[away]
            self.step = send(self.mail.at[2 * away + core], self.chip_in, to_chip)

        def wait(self):
            self.step.wait_recv()
            value = self.mail[me].astype(F32) + self.core_in[chip].astype(F32)
            return value + self.chip_in[...].astype(F32)

    lanes = 2 * part

    class Reduce:
        def __init__(self, at, top, length):
            self.group = getattr(r, GROUPS[at // 2])
            self.at = at
            self.rows = pl.ds(top, length)
            self.cols = pl.ds(at % 2 * lanes, lanes)
            self.order = ORDERS[at]
            self.step = 0

        def index(self, last):
            spots = [slice(None)] * 3
            for bit in self.order[: self.step]:
                spots[2 - bit] = bits[bit]
            bit = self.order[self.step]
            spots[2 - bit] = last(bits[bit])
            return tuple(spots) + (self.rows, self.cols)

        def start(self):
            inbox = (r.in_half, r.in_quarter, r.in_eighth)[self.step]
            inbox = inbox.at[(self.at,) + (slice(None),) * (2 - self.step) + (self.rows,)]
            away = self.index(lambda bit: 1 - bit)
            self.copy = send(self.group.at[away], inbox, peers_dp[self.order[self.step]])
            self.inbox = inbox

        def next(self):
            self.copy.wait_recv()
            keep = self.index(lambda bit: bit)
            value = self.group[keep] + self.inbox[...]
            if self.step < 2:
                self.group[keep] = value
                self.step += 1
                self.start()
            else:
                r.b_sums[self.at, me, self.rows, :] = value
                spot = lambda who: r.b_sums.at[self.at, who, self.rows]
                if self.at < STRAIGHT:
                    self.gather = Gather(spot(me), spot)
                else:
                    self.copies = [send(spot(me), spot(me), peer) for peer in peers + [to_far]]

        def relay(self):
            self.gather.relay()

        def wait(self):
            if self.at < STRAIGHT:
                self.gather.wait()
            else:
                for copy in self.copies:
                    copy.wait_recv()
            kept.ended[self.at] = kept.ended.get(self.at, 0) + 1
            if kept.ended[self.at] == CUTS[self.at // 2]:
                store(r.b_sums.at[self.at], r.o_sums.at[self.at])

    def put(group, at, value):
        ref = getattr(r, GROUPS[group])
        value = value.astype(BF16)
        if direct:
            value = value.reshape(2, 2, 2, share, value.shape[-1])
            ref[:, :, :, :, at : at + value.shape[-1]] = value
        else:
            ref[:, at : at + value.shape[-1]] = value

    def feed_up(c, rows):
        if once(W_CO):
            ready(get_co, *([] if direct else get_fi))
        kept.to_cross[c].wait()
        mixed = joined(r.cross_parts, c)
        r.cross_mixed[rows, :] = mixed
        after = r.after[rows, :] + mm(mixed, r.all_co[...])
        r.after[rows, :] = after
        normed, rate = normalize(after)
        r.n_feed[rows, :] = normed.astype(BF16)
        r.r_feed[rows, :] = rate
        hidden = (normed * gain_f + shift_f).astype(BF16)
        r.h_feed[rows, :] = hidden
        upward = mm(hidden, r.own_fi[...])
        bell = 0.5 + 0.5 * lax.erf(upward * 2.0**-0.5)
        r.active[rows, :] = (upward * bell).astype(BF16)
        kept.slope[c] = bell + upward * jnp.exp(-0.5 * upward * upward) * 0.3989422804014327

    def feed_back(c, rows):
        if once(W_FO):
            ready(*get_fo)
        out_wait()
        normed, slope = r.n_feed[rows, :].astype(F32), kept.slope[c]
        grad_up = (mm_t(r.grad_out[rows, :], r.own_fo[...]) * slope).astype(BF16)
        r.grad_up[rows, :] = grad_up
        back = mm_t(grad_up, r.own_fi[...])
        add(4, back * normed)
        add(5, back)
        kept.total[c] = Total(c, back)

    def layer_chunk(c, rows):
        if once(W_FO):
            ready(*get_fo)
        value = mm(r.active[rows, :], r.own_fo[...]).astype(BF16)
        r.layer_mail[2 * c : 2 * c + 2] = value.reshape(2, span, width)

    @task(LAYER_SEND)
    def _():
        kept.layer = Scatter(r.layer_mail, r.layer_core, r.layer_chip)

    @task(LAYER_SECOND)
    def _():
        kept.layer.second()

    @task(LAYER_OUT)
    def _():
        r.b_layer[...] = r.after[own_span, :] + kept.layer.wait()
        store(r.b_layer, r.o_layer)

    @task(GRAD_FO)
    def _():
        out_wait()
        put(0, 0, t_mm(r.active[...], r.grad_out[...]))

    @task(GRAD_FI)
    def _():
        put(1, 0, t_mm(r.h_feed[...], r.grad_up[...]))

    def cross_before(c, rows):
        grad = kept.total[c].wait()
        normed = r.n_feed[rows, :].astype(F32)
        grad = r.grad_out[rows, :].astype(F32) + norm_back(grad, gain_f, normed, r.r_feed[rows, :])
        r.grad_row[rows, :] = grad
        low = grad.astype(BF16)
        r.grad_cross[rows, :] = low
        to_heads(mm_t(low, r.all_co[own_rows, :]).astype(BF16), r.grad_mix, rows)

    def cross_back(c, rows):
        heads = attend_back(
            r.cq, r.mk, r.mv, r.grad_mix, r.cross_weights, r.cross_mix,
            r.grad_mk, r.grad_mv, rows, src_full, c == 0,
        )
        r.grad_cross_rows[rows, :] = jnp.concatenate(heads, axis=1)
        kept.to_rows[c] = gather_columns(r.row_parts, c, heads)

    @task(MEMORY_TERMS)
    def _():
        mk_t = r.grad_mk[...].reshape(part, src_full)
        mv_t = r.grad_mv[...].reshape(part, src_full)
        terms = mm_t(place(mk_t.T.astype(BF16)), r.win_ck[...]) + mm_t(
            place(mv_t.T.astype(BF16)), r.win_cv[...]
        )
        r.mem_mail[...] = terms.astype(BF16).reshape(seq, src_span, width)
        kept.memory = Scatter(r.mem_mail, r.mem_core, r.mem_chip)

    @task(MEMORY_SECOND)
    def _():
        kept.memory.second()

    @task(MEMORY_OUT)
    def _():
        r.b_memory[...] = kept.memory.wait()
        store(r.b_memory, r.o_memory)

    @task(GRAD_CK)
    def _():
        put(2, part, mm(r.grad_mk[...].reshape(part, src_full).astype(BF16), r.mem[...]).T)

    @task(GRAD_CV)
    def _():
        put(2, 2 * part, mm(r.grad_mv[...].reshape(part, src_full).astype(BF16), r.mem[...]).T)

    @task(GRAD_CO)
    def _():
        put(2, 0, pick(t_mm(r.cross_mixed[...], r.grad_cross[:, window])))

    @task(GRAD_CQ)
    def _():
        put(2, 3 * part, t_mm(r.h_cross[...], r.grad_cross_rows[...]))

    def self_before(c, rows):
        kept.to_rows[c].wait()
        grad = mm_t(joined(r.row_parts, c), r.all_cq[...])
        normed = r.n_cross[rows, :].astype(F32)
        add(2, grad * normed)
        add(3, grad)
        grad = r.grad_row[rows, :] + norm_back(grad, gain_c, normed, r.r_cross[rows, :])
        r.grad_row[rows, :] = grad
        to_heads(mm_t(grad.astype(BF16), r.all_so[own_rows, :]).astype(BF16), r.grad_mix, rows)

    def self_back(c, rows):
        heads = attend_back(
            r.q, r.k, r.v, r.grad_mix, r.self_weights, r.self_mix,
            r.grad_k, r.grad_v, rows, rows.stop, c == CHUNKS - 1, own_head,
        )
        r.grad_self_rows[rows, :] = jnp.concatenate(heads, axis=1)

    def put_self(at, value):
        if not direct:
            put(3, at * part, value)
        elif at in (1, 2):
            put(3, (at - 1) * part, value)
        else:
            value = value.astype(BF16).reshape(2, 2, 2, share, part)
            tall = share // 2
            packed = jnp.concatenate([value[:, :, :, :tall], value[:, :, :, tall:]], axis=4)
            top = 0 if at == 0 else tall
            r.g_self[:, :, :, top : top + tall, lanes:] = packed

    @task(GRAD_SO)
    def _():
        put_self(0, pick(t_mm(r.self_mixed[...], r.grad_row[:, window].astype(BF16))))

    @task(GRAD_SQ)
    def _():
        put_self(1, t_mm(r.h_attend[...], r.grad_self_rows[...]))

    @task(GRAD_SK)
    def _():
        put_self(2, mm(r.grad_k[...].reshape(part, full).astype(BF16), r.h_attend[...]).T)

    @task(GRAD_SV)
    def _():
        put_self(3, mm(r.grad_v[...].reshape(part, full).astype(BF16), r.h_attend[...]).T)

    @task(TOKEN_TERMS)
    def _():
        k_t = r.grad_k[...].reshape(part, full)
        v_t = r.grad_v[...].reshape(part, full)
        back = (
            mm_t(place(r.grad_self_rows[...]), r.win_sq[:, own_window])
            + mm_t(place(k_t.T.astype(BF16)), r.win_sk[:, own_window])
            + mm_t(place(v_t.T.astype(BF16)), r.win_sv[:, own_window])
        )
        add(0, back * r.n_attend[...].astype(F32))
        add(1, back)
        r.tok_mail[...] = back.astype(BF16).reshape(seq, span, width)
        kept.tokens = Scatter(r.tok_mail, r.tok_core, r.tok_chip)

    @task(TOKEN_SECOND)
    def _():
        kept.tokens.second()

    @task(TOKEN_OUT)
    def _():
        normed, rate = normalize(r.row[own_span, :].astype(F32))
        grad = kept.tokens.wait()
        r.b_tokens[...] = r.grad_row[own_span, :] + norm_back(grad, gain_a, normed, rate)
        store(r.b_tokens, r.o_tokens)

    class Stats:
        def __init__(self):
            shared = jnp.where(me == 0, 1.0, 0.0)
            rows = stats[:2] + [row * shared for row in stats[2:4]] + stats[4:]
            self.value = jnp.concatenate(rows + [jnp.zeros((2, width), F32)], axis=0)
            self.step = 0
            r.o_stats[...] = self.value

        def start(self):
            r.stat_out[self.step] = self.value
            peer = (peers + peers_dp)[self.step]
            self.copy = send(r.stat_out.at[self.step], r.stat_in.at[self.step], peer)

        def next(self):
            self.copy.wait_recv()
            self.value = self.value + r.stat_in[self.step]
            self.step += 1
            if self.step < 5:
                self.start()
            else:
                r.o_stats[...] = self.value

    @task(NORMS_SEND)
    def _():
        kept.stats = Stats()
        if direct:
            kept.stats.start()

    if direct:
        for level in range(5):
            tasks[NORMS_STEP, level] = lambda: kept.stats.next()

    for c, rows in enumerate(chunks):
        for name, function in (
            (SELF, self_chunk),
            (ROWS, cross_rows),
            (CROSS, cross_chunk),
            (FEED_UP, feed_up),
            (FEED_BACK, feed_back),
            (LAYER, layer_chunk),
            (CROSS_GRAD, cross_before),
            (CROSS_BACK, cross_back),
            (SELF_GRAD, self_before),
            (SELF_BACK, self_back),
        ):
            tasks[name, c] = functools.partial(function, c, rows)
        tasks[CROSS_RELAY, c] = lambda c=c: kept.to_cross[c].relay()
        tasks[ROWS_RELAY, c] = lambda c=c: kept.to_rows[c].relay()
        tasks[TOTAL_SECOND, c] = lambda c=c: kept.total[c].second()
        tasks[TOTAL_THIRD, c] = lambda c=c: kept.total[c].third()

    if direct:
        for at in range(8):
            cuts = CUTS[at // 2]
            for cut in range(cuts):
                one = Reduce(at, cut * (share // cuts), share // cuts)
                for level, function in enumerate(
                    (one.start, one.next, one.next, one.next, one.relay, one.wait)
                ):
                    tasks[at, cut, level] = function

    for name in SCHEDULE:
        if name in tasks:
            tasks[name]()
    finish(list(busy))
    ready(*stores)


def row_call(seq, span, src_span, width, part, units, direct, operands):
    full, src_full = span * seq, src_span * seq
    count, size = part // HEAD_DIM, full // CHUNKS
    half = size // 2
    shapes = dict(
        row=((full, width), BF16),
        mem=((src_full, width), BF16),
        grad_out=((full, width), BF16),
        win_sq=((width, 2 * part), BF16),
        win_sk=((width, 2 * part), BF16),
        win_sv=((width, 2 * part), BF16),
        win_ck=((width, WINDOW), BF16),
        win_cv=((width, WINDOW), BF16),
        all_so=((width, width), BF16),
        all_cq=((width, width), BF16),
        all_co=((width, width), BF16),
        own_fi=((width, units), BF16),
        own_fo=((units, width), BF16),
        self_bias=((full, full), F32),
        target_col=((full, 1), F32),
        cross_code=((1, src_full), F32),
        n_attend=((full, width), BF16),
        n_cross=((full, width), BF16),
        n_feed=((full, width), BF16),
        r_cross=((full, 1), F32),
        r_feed=((full, 1), F32),
        h_attend=((full, width), BF16),
        h_cross=((full, width), BF16),
        h_feed=((full, width), BF16),
        after=((full, width), F32),
        grad_row=((full, width), F32),
        q=((2 * count, full, HEAD_DIM), BF16),
        k=((2 * count, full, HEAD_DIM), BF16),
        v=((2 * count, full, 2 * HEAD_DIM), BF16),
        cq=((count, full, HEAD_DIM), BF16),
        mk=((count, src_full, HEAD_DIM), BF16),
        mv=((count, src_full, 2 * HEAD_DIM), BF16),
        grad_mix=((count, full, HEAD_DIM), BF16),
        self_weights=((count * full, full), BF16),
        cross_weights=((count * full, src_full), BF16),
        self_mix=((count, full, 2 * HEAD_DIM), F32),
        cross_mix=((count, full, 2 * HEAD_DIM), F32),
        grad_k=((count, HEAD_DIM, full), F32),
        grad_v=((count, HEAD_DIM, full), F32),
        grad_mk=((count, HEAD_DIM, src_full), F32),
        grad_mv=((count, HEAD_DIM, src_full), F32),
        cross_parts=((CHUNKS, seq, size + half, 2 * HEAD_DIM), BF16),
        row_parts=((CHUNKS, seq, size + half, 2 * HEAD_DIM), BF16),
        self_mixed=((full, width), BF16),
        cross_mixed=((full, width), BF16),
        active=((full, units), BF16),
        grad_up=((full, units), BF16),
        grad_cross=((full, width), BF16),
        grad_cross_rows=((full, part), BF16),
        grad_self_rows=((full, part), BF16),
        sum_send=((CHUNKS, size, width), BF16),
        sum_core=((CHUNKS, half, width), BF16),
        sum_mid=((CHUNKS, half, width), BF16),
        sum_chip=((CHUNKS, half, width), BF16),
        sum_full=((CHUNKS, size, width), BF16),
        layer_mail=((seq, span, width), BF16),
        layer_core=((2, span, width), BF16),
        layer_chip=((span, width), BF16),
        tok_mail=((seq, span, width), BF16),
        tok_core=((2, span, width), BF16),
        tok_chip=((span, width), BF16),
        b_layer=((span, width), F32),
        b_tokens=((span, width), F32),
        b_memory=((src_span, width), F32),
        mem_mail=((seq, src_span, width), BF16),
        mem_core=((2, src_span, width), BF16),
        mem_chip=((src_span, width), BF16),
    )
    group = (width, 4 * part)
    if direct:
        blocks, share = 8, width // 8
        lanes = 2 * part
        group = (2, 2, 2, share, 4 * part)
        shapes.update({name: (group, BF16) for name in GROUPS})
        shapes.update(
            in_half=((8, 2, 2, share, lanes), BF16),
            in_quarter=((8, 2, share, lanes), BF16),
            in_eighth=((8, share, lanes), BF16),
            b_sums=((8, seq, share, lanes), BF16),
            stat_out=((5, 8, width), F32),
            stat_in=((5, 8, width), F32),
        )
    names = list(shapes) + SEMAPHORES
    scratch = [pltpu.VMEM(shape, dtype) for shape, dtype in shapes.values()]
    scratch += [pltpu.SemaphoreType.DMA((80,)), pltpu.SemaphoreType.DMA((224,)), pltpu.SemaphoreType.DMA((224,))]
    hbm = pl.BlockSpec(memory_space=pl.ANY)
    vmem = pl.BlockSpec(memory_space=pltpu.VMEM)
    smem = pl.BlockSpec(memory_space=pltpu.SMEM)
    outs = [((span, width), F32), ((span, width), F32), ((src_span, width), F32), ((8, width), F32)]
    out_specs = [hbm] * 3 + [vmem]
    if direct:
        outs += [((8, seq, share, lanes), BF16)]
        out_specs += [hbm]
    else:
        outs += [(group, BF16)] * 4
        out_specs += [vmem] * 4
    return pl.pallas_call(
        functools.partial(row_kernel, names, seq, direct),
        out_shape=[jax.ShapeDtypeStruct(s, t) for s, t in outs],
        in_specs=[hbm] * 3 + [vmem] * 2 + [smem] + [hbm] * 10 + [vmem] * 6,
        out_specs=out_specs,
        scratch_shapes=scratch,
        compiler_params=pltpu.CompilerParams(
            collective_id=0, has_side_effects=True, vmem_limit_bytes=64 * 2**20 - 2**17
        ),
    )(*operands)


def final_kernel(seq, dp, layer, tokens, memory, stats, sums, *refs):
    outs, norms, got, passed, built = refs[:13], refs[13:19], refs[19], refs[20:23], refs[23:33]
    in_sems, out_sems = refs[33:]
    sources = [(sums.at[pl.ds(2 * g, 2)], got.at[pl.ds(2 * g, 2)]) for g in range(4)]
    sources += list(zip((memory, layer, tokens), (passed[2], passed[0], passed[1])))
    loads = [pltpu.make_async_copy(*pair, in_sems.at[i]) for i, pair in enumerate(sources)]
    stores = [
        pltpu.make_async_copy(src, dst, out_sems.at[i])
        for i, (src, dst) in enumerate(zip(passed + built, outs))
    ]
    for copy in loads:
        copy.start()
    share, lanes = sums.shape[2:]
    part = lanes // 2
    sq, sk, sv, so, cq, ck, cv, co, fi, fo = built
    width = stats.shape[1]
    back = lax.rem(width - lax.axis_index("dp") * share, width)
    own = pltpu.roll(stats[...], back, 1)[:, :share]
    for i, out in enumerate(norms):
        out[...] = own[i]
    unit = fo.shape[0] // seq
    loads[0].wait()
    for s in range(seq):
        for at in range(2):
            fo[s * unit : (s + 1) * unit, at * lanes : (at + 1) * lanes] = got[at, s].astype(F32)
    stores[12].start()
    loads[1].wait()
    for at in range(2):
        wide = [got[2 + at, s].astype(F32) for s in range(seq)]
        for b in range(dp // 2):
            block = [w[:, b * unit : (b + 1) * unit] for w in wide]
            start = (at * (dp // 2) + b) * seq * unit
            fi[:, start : start + seq * unit] = jnp.concatenate(block, 1)
    stores[11].start()
    loads[2].wait()
    loads[3].wait()
    for i, (out, spot) in enumerate(zip((co, ck, cv, cq, sq, sk), (10, 8, 9, 7, 3, 4))):
        start = i % 2 * part
        block = [got[4 + i // 2, s].astype(F32)[:, start : start + part] for s in (0, 2, 1, 3)]
        out[...] = jnp.concatenate(block, 1)
        stores[spot].start()
    tall = share // 2
    for out, top, spot in ((so, 0, 6), (sv, tall, 5)):
        block = [got[7, s].astype(F32)[top : top + tall] for s in (0, 2, 1, 3)]
        for side in range(2):
            pieces = [piece[:, side * part : (side + 1) * part] for piece in block]
            out[side * tall : (side + 1) * tall, :] = jnp.concatenate(pieces, 1)
        stores[spot].start()
    for copy, place in zip(loads[4:], (2, 0, 1)):
        copy.wait()
        stores[place].start()
    for copy in stores:
        copy.wait()


def final_call(seq, dp, layer, tokens, memory, stats, sums):
    share, width = sums.shape[2], stats.shape[1]
    feed = sums.shape[3] * 2 * seq
    hbm = pl.BlockSpec(memory_space=pl.ANY)
    vmem = pl.BlockSpec(memory_space=pltpu.VMEM)
    shapes = [layer.shape, tokens.shape, memory.shape] + [(share, width)] * 8
    shapes += [(share, feed), (feed // dp, width)] + [(share,)] * 6
    return pl.pallas_call(
        functools.partial(final_kernel, seq, dp),
        out_shape=[jax.ShapeDtypeStruct(shape, F32) for shape in shapes],
        in_specs=[hbm] * 3 + [vmem] + [hbm],
        out_specs=[hbm] * 13 + [vmem] * 6,
        scratch_shapes=[pltpu.VMEM(sums.shape, BF16)]
        + [pltpu.VMEM(shape, F32) for shape in shapes[:13]]
        + [pltpu.SemaphoreType.DMA((7,)), pltpu.SemaphoreType.DMA((13,))],
        compiler_params=pltpu.CompilerParams(vmem_limit_bytes=64 * 2**20 - 2**17),
    )(layer, tokens, memory, stats, sums)


def swap(value, axis, bit):
    size = lax.axis_size(axis)
    return lax.ppermute(value, axis, [(i, i ^ bit) for i in range(size)])


def scatter_sum(value, bits):
    index = lax.axis_index("dp")
    size = lax.axis_size("dp")
    levels = size.bit_length() - 1
    blocks = value.reshape((2,) * levels + value.shape[1:])
    left = list(range(levels))[::-1]
    for bit in bits:
        at = left.index(bit)
        mine = (index >> bit) & 1
        keep = lax.dynamic_index_in_dim(blocks, mine, at, keepdims=False)
        away = lax.dynamic_index_in_dim(blocks, 1 - mine, at, keepdims=False)
        left.pop(at)
        got = swap(away.astype(BF16), "dp", 1 << bit)
        blocks = keep.astype(F32) + got.astype(F32)
    return blocks


def shards(
    tokens,
    memory,
    target_segments,
    memory_segments,
    pad_counts,
    out_grad,
    self_query,
    self_key,
    self_value,
    self_out,
    cross_query,
    cross_key,
    cross_value,
    cross_out,
    feed_in,
    feed_out,
    gain_attend,
    shift_attend,
    gain_cross,
    shift_cross,
    gain_feed,
    shift_feed,
):
    seq, dp = lax.axis_size("seq"), lax.axis_size("dp")
    me = lax.axis_index("seq")
    span, width = tokens.shape[1:]
    part = width // seq
    feed = feed_in.shape[1]
    unit = feed // dp // seq
    direct = dp == 8 and unit == width // dp and unit % 16 == 0
    fi, fo = feed_in, feed_out
    if not direct:
        fi = lax.dynamic_index_in_dim(fi.reshape(width, dp, seq, unit), me, 2, keepdims=False)
        fi = fi.reshape(width, dp * unit)
        fo = lax.dynamic_index_in_dim(fo.reshape(dp, seq, unit, width), me, 1, keepdims=False)
        fo = fo.reshape(dp * unit, width)
    operands = (
        tokens[0], memory[0], out_grad[0], target_segments, memory_segments, pad_counts,
        self_query, self_key, self_value, self_out, cross_query, cross_key, cross_value, cross_out,
        fi, fo, gain_attend, shift_attend, gain_cross, shift_cross, gain_feed, shift_feed,
    )
    results = row_call(seq, span, memory.shape[1], width, part, dp * unit, direct, operands)
    if direct:
        results = final_call(seq, dp, *results)
        return tuple(value[None] for value in results[:3]) + tuple(results[3:])
    layer_out, tokens_grad, memory_grad, stats, g_fo, g_fi, g_cross, g_self = results
    gather = lambda v, axis: lax.all_gather(v, "seq", axis=axis, tiled=True)

    levels = dp.bit_length() - 1
    up = list(range(levels))
    first, second = up, up[1:] + up[:1]
    share = width // dp
    split = lambda v: v.reshape(dp, share, -1)
    groups = ((split(g_fo), first), (split(g_fi), second), (split(g_cross), first), (split(g_self), second))
    summed = [gather(scatter_sum(v, bits).astype(BF16)[None], 0) for v, bits in groups]
    whole_fo = summed[0].reshape(seq * share, width).astype(F32)
    whole_fi = (
        summed[1].reshape(seq, share, dp, unit).transpose(1, 2, 0, 3).reshape(share, feed)
    ).astype(F32)

    def whole(group, at):
        block = group[:, :, at * part : (at + 1) * part]
        block = block.reshape(2, 2, share, part).transpose(2, 1, 0, 3)
        return block.reshape(share, width).astype(F32)

    co, ck, cv, cq = (whole(summed[2], at) for at in range(4))
    so, sq, sk, sv = (whole(summed[3], at) for at in range(4))
    stats = lax.psum(stats, ("seq", "dp"))
    norm_part = lax.dynamic_slice_in_dim(stats, lax.axis_index("dp") * share, share, 1)
    return (
        layer_out[None],
        tokens_grad[None],
        memory_grad[None],
        sq,
        sk,
        sv,
        so,
        cq,
        ck,
        cv,
        co,
        whole_fi,
        whole_fo,
    ) + tuple(norm_part[i] for i in range(6))


def solution(mesh):
    rows = P("dp", "seq", None)
    in_specs = (rows, rows, P("dp", None), P("dp", None), P("dp", None), rows) + (P(),) * 16
    out_specs = (rows,) * 3 + (P("dp", None),) * 10 + (P("dp"),) * 6
    return jax.shard_map(shards, mesh=mesh, in_specs=in_specs, out_specs=out_specs, check_vma=False)
```

profile of v0, /device:TPU:0, one launch (start us, length us, event | category | flops | bytes accessed | tf_op | source)
XLA Modules:
  0.0 103.4 jit_solution(17612315939085251166)
XLA Ops:
  0.7 97.3 %shard_map.357 = (f32[128,768]{1,0:T(8,128)}, f32[128,768]{1,0:T(8,128)}, f32[256,768]{1,0:T(8,128)}, f32[8,768]{1,0:T(8,128)}, bf16[8,4,96,384]{3,2,1,0:T(8,128)(2,1)}) custom-call(bf16[128,768]{1,0:T(8,128)(2,1)} %bitcast.7, bf16[256,768]{1,0:T(8,128)(2,1)} %bitcast.6, bf16[128,768]{1,0:T(8,128)(2,1)} %bitcast.8, s32[1,512]{1,0:T(1,128)} %refs_3_.1, ...), custom_call_target="tpu_custom_call" | custom-call | tf_op jit(solution)/shard_map/pallas_call | solution.py:931
  97.9 5.3 %shard_map.358 = (f32[128,768]{1,0:T(8,128)}, f32[128,768]{1,0:T(8,128)}, f32[256,768]{1,0:T(8,128)}, f32[96,768]{1,0:T(8,128)}, f32[96,768]{1,0:T(8,128)}, /*in...) custom-call(f32[128,768]{1,0:T(8,128)} %get-tuple-element.43.layer, ...), custom_call_target="tpu_custom_call" | custom-call | tf_op jit(solution)/shard_map/pallas_call | solution.py:1005
where the time goes:
time: 104 us; the launch traced here: 103 us
  Pallas kernels  103 us (99%)
    pallas_call x1, Pallas kernels, row_call(): pl.pallas_call(functools.partial(row_kernel, names, seq, direct), out_sha...  97.3 us
    pallas_call x1, Pallas kernels, final_call(): pl.pallas_call(functools.partial(final_kernel, seq, dp), out_shape=[jax.S...  5.29 us

commit v1 on v0

--- a/solution.py
+++ b/solution.py
@@ -53,9 +53,9 @@
 SEMAPHORES = ["load_sem", "send_sem", "recv_sem"]
 GROUPS = ["g_fo", "g_fi", "g_cross", "g_self"]
 ALONG, ACROSS, MIXED, TURNED = (1, 2, 0), (0, 1, 2), (1, 0, 2), (0, 2, 1)
-ORDERS = (ACROSS, ALONG, ALONG, ACROSS, ACROSS, ACROSS, ACROSS, ACROSS)
+ORDERS = (MIXED, ACROSS, ACROSS, ALONG, ACROSS, ACROSS, ACROSS, ACROSS)
 STRAIGHT = 6
-CUTS = (2, 1, 1, 6)
+CUTS = (1, 1, 2, 6)
 (
     OWN_FI, TOKENS_NEAR, TOKENS_MIDDLE, TOKENS_FAR, MEMORY_NEAR, MEMORY_MIDDLE, MEMORY_FAR, TOKENS_RELAY, MEMORY_RELAY,
     COTANGENT_SEND, COTANGENT_RELAY, LAYER_SEND, LAYER_SECOND, LAYER_OUT, MEMORY_TERMS,
@@ -68,28 +68,28 @@
 ) = range(100, 115)
 OUT, W_SO, W_CO, W_FO = range(4)
 SCHEDULE = [
-    OWN_FI, TOKENS_NEAR, MEMORY_NEAR, TOKENS_RELAY, TOKENS_MIDDLE, TOKENS_FAR, (SELF, 1), (SELF, 0),
-    (ROWS, 1), COTANGENT_SEND, (ROWS, 0), MEMORY_RELAY, MEMORY_MIDDLE, MEMORY_FAR, (CROSS, 0),
-    (CROSS, 1), COTANGENT_RELAY, (CROSS_RELAY, 0), (FEED_UP, 0), (CROSS_RELAY, 1), (FEED_BACK, 0),
-    (FEED_UP, 1), (TOTAL_SECOND, 0), GRAD_FO, (LAYER, 1), (1, 0, 0), (0, 0, 0), (FEED_BACK, 1),
-    GRAD_FI, (3, 0, 0), (2, 0, 0), (TOTAL_SECOND, 1), (LAYER, 0), LAYER_SEND, (0, 1, 0), (1, 1, 0),
-    (TOTAL_THIRD, 0), LAYER_SECOND, (1, 0, 1), (0, 0, 1), (CROSS_GRAD, 0), (CROSS_BACK, 0),
-    (TOTAL_THIRD, 1), (CROSS_GRAD, 1), GRAD_CO, (CROSS_BACK, 1), GRAD_CK, (4, 0, 0), (ROWS_RELAY, 0),
-    (1, 1, 1), GRAD_CQ, LAYER_OUT, (1, 0, 2), (3, 0, 1), (0, 1, 1), GRAD_CV, (0, 0, 2), (5, 0, 0),
-    MEMORY_TERMS, (ROWS_RELAY, 1), (2, 0, 1), (SELF_GRAD, 0), (1, 1, 2), MEMORY_SECOND, (SELF_GRAD, 1),
-    GRAD_SO, (7, 0, 0), (3, 0, 2), (4, 0, 1), (SELF_BACK, 1), (SELF_BACK, 0), GRAD_SK, GRAD_SV,
-    (7, 4, 0), (7, 1, 0), (7, 2, 0), TOKEN_TERMS, (7, 3, 0), (0, 1, 2), (5, 0, 1), (1, 0, 3),
-    NORMS_SEND, GRAD_SQ, TOKEN_SECOND, (NORMS_STEP, 0), (6, 0, 0), (7, 0, 1), (2, 0, 2), (4, 0, 2),
-    MEMORY_OUT, (7, 5, 0), (7, 4, 1), (0, 0, 3), (6, 1, 0), (6, 2, 0), (6, 3, 0), (6, 4, 0), (6, 5, 0),
-    (3, 0, 3), (1, 0, 4), (7, 1, 1), (1, 1, 3), (7, 2, 1), (1, 0, 5), (0, 1, 3), (7, 3, 1), (5, 0, 2),
-    (7, 0, 2), (6, 0, 1), TOKEN_OUT, (NORMS_STEP, 1), (2, 0, 3), (4, 0, 3), (7, 4, 2), (0, 0, 4),
-    (7, 1, 2), (7, 5, 1), (7, 2, 2), (0, 0, 5), (7, 3, 2), (6, 1, 1), (3, 0, 4), (1, 1, 4), (6, 2, 1),
-    (3, 0, 5), (0, 1, 4), (5, 0, 3), (6, 0, 2), (6, 3, 1), (1, 1, 5), (7, 0, 3), (0, 1, 5), (7, 4, 3),
-    (6, 4, 1), (7, 5, 2), (7, 1, 3), (2, 0, 4), (7, 2, 3), (6, 5, 1), (6, 1, 2), (7, 3, 3),
-    (NORMS_STEP, 2), (2, 0, 5), (6, 2, 2), (4, 0, 4), (6, 3, 2), (6, 0, 3), (6, 4, 2), (4, 0, 5),
-    (5, 0, 4), (7, 5, 3), (7, 0, 5), (6, 5, 2), (7, 4, 5), (5, 0, 5), (6, 1, 3), (NORMS_STEP, 3),
-    (7, 1, 5), (7, 2, 5), (6, 2, 3), (7, 3, 5), (6, 3, 3), (6, 0, 5), (6, 4, 3), (7, 5, 5), (6, 5, 3),
-    (6, 1, 5), (6, 2, 5), (NORMS_STEP, 4), (6, 3, 5), (6, 4, 5), (6, 5, 5),
+    TOKENS_NEAR, OWN_FI, MEMORY_NEAR, TOKENS_RELAY, TOKENS_MIDDLE, TOKENS_FAR, (SELF, 1), (SELF, 0),
+    COTANGENT_SEND, (ROWS, 1), MEMORY_RELAY, (ROWS, 0), MEMORY_MIDDLE, MEMORY_FAR, (CROSS, 0),
+    COTANGENT_RELAY, (CROSS, 1), (CROSS_RELAY, 0), (FEED_UP, 0), (CROSS_RELAY, 1), (FEED_BACK, 0),
+    (FEED_UP, 1), (TOTAL_SECOND, 0), GRAD_FO, (1, 0, 0), (0, 0, 0), (FEED_BACK, 1), GRAD_FI,
+    (TOTAL_SECOND, 1), (2, 0, 0), (3, 0, 0), (LAYER, 1), (TOTAL_THIRD, 0), (LAYER, 0), LAYER_SEND,
+    (CROSS_GRAD, 0), (CROSS_BACK, 0), (TOTAL_THIRD, 1), (1, 0, 1), (0, 0, 1), LAYER_SECOND,
+    (CROSS_GRAD, 1), (CROSS_BACK, 1), GRAD_CV, GRAD_CQ, (5, 0, 0), (3, 0, 1), MEMORY_TERMS, (5, 1, 0),
+    GRAD_CO, (ROWS_RELAY, 0), GRAD_CK, (0, 0, 2), (2, 0, 1), (4, 0, 0), MEMORY_SECOND, (ROWS_RELAY, 1),
+    (1, 0, 2), (4, 1, 0), (SELF_GRAD, 0), (SELF_GRAD, 1), (5, 0, 1), GRAD_SO, (SELF_BACK, 1),
+    (5, 1, 1), (7, 1, 0), (SELF_BACK, 0), (4, 0, 1), (2, 0, 2), GRAD_SK, (0, 0, 3), (7, 0, 0),
+    (7, 2, 0), GRAD_SQ, (6, 0, 0), (5, 0, 2), TOKEN_TERMS, (1, 0, 3), (6, 1, 0), (5, 1, 2), (7, 1, 1),
+    GRAD_SV, (7, 5, 0), TOKEN_SECOND, (7, 0, 1), (4, 1, 1), NORMS_SEND, (4, 0, 2), (6, 2, 0),
+    (7, 2, 1), (7, 3, 0), (6, 3, 0), (7, 1, 2), (7, 0, 2), (NORMS_STEP, 0), (6, 0, 1), (7, 4, 0),
+    (7, 5, 1), (2, 0, 3), (6, 4, 0), (5, 0, 3), LAYER_OUT, (3, 0, 2), (6, 2, 1), (4, 1, 2), (6, 3, 1),
+    (4, 0, 3), (6, 1, 1), (5, 1, 3), (6, 5, 0), (7, 3, 1), (7, 1, 3), (6, 0, 2), (6, 2, 2), (6, 4, 1),
+    (7, 5, 2), (7, 4, 1), (7, 0, 3), (NORMS_STEP, 1), (4, 1, 3), (6, 3, 2), (6, 1, 2), (3, 0, 3),
+    (7, 2, 2), (6, 5, 1), (7, 3, 2), (5, 0, 4), (6, 2, 3), (6, 0, 3), (6, 4, 2), (NORMS_STEP, 2),
+    (7, 5, 3), (1, 0, 4), (2, 0, 4), (7, 4, 2), (4, 1, 4), (6, 3, 3), (0, 0, 4), (6, 5, 2), (6, 1, 3),
+    (7, 2, 3), (4, 1, 5), (5, 1, 4), (7, 3, 3), (3, 0, 4), (6, 4, 3), (NORMS_STEP, 3), TOKEN_OUT,
+    (6, 0, 5), (7, 4, 3), MEMORY_OUT, (6, 5, 3), (7, 5, 5), (2, 0, 5), (6, 1, 5), (7, 1, 5), (5, 0, 5),
+    (6, 2, 5), (0, 0, 5), (7, 2, 5), (4, 0, 4), (7, 0, 5), (4, 0, 5), (3, 0, 5), (6, 3, 5),
+    (NORMS_STEP, 4), (5, 1, 5), (1, 0, 5), (7, 3, 5), (6, 4, 5), (7, 4, 5), (6, 5, 5),
 ]
 
 
@@ -820,8 +820,13 @@
                 ):
                     tasks[at, cut, level] = function
 
+    begun, late = [], False
     for name in SCHEDULE:
         if name in tasks:
+            late = late or name == TOKEN_TERMS
+            begun.append(list(busy))
+            if late:
+                finish([copy for copy in busy if any(copy is old for old in begun[-24])][:8])
             tasks[name]()
     finish(list(busy))
     ready(*stores)

time: 104 us -> 102 us (0.981)
  Pallas kernels: 103 us -> 101 us
    pallas_call x1, Pallas kernels: 97.3 us -> 95.7 us  [row_call(): pl.pallas_call(functools.partial(row_kernel, names, seq, direct), out_sha...]
where the time goes in v1:
time: 102 us
  Pallas kernels  101 us (99%)
    pallas_call x1, Pallas kernels, row_call(): pl.pallas_call(functools.partial(row_kernel, names, seq, direct), out_sha...  95.7 us
    pallas_call x1, Pallas kernels, final_call(): pl.pallas_call(functools.partial(final_kernel, seq, dp), out_shape=[jax.S...  5.29 us

profile of v1, /device:TPU:0, one launch (start us, length us, event | category | flops | bytes accessed | tf_op | source)
XLA Modules:
  0.0 101.8 jit_solution(4622139893672098022)
XLA Ops:
  0.7 95.7 %shard_map.357 = (f32[128,768]{1,0:T(8,128)}, f32[128,768]{1,0:T(8,128)}, f32[256,768]{1,0:T(8,128)}, f32[8,768]{1,0:T(8,128)}, bf16[8,4,96,384]{3,2,1,0:T(8,128)(2,1)}) custom-call(bf16[128,768]{1,0:T(8,128)(2,1)} %bitcast.7, bf16[256,768]{1,0:T(8,128)(2,1)} %bitcast.6, bf16[128,768]{1,0:T(8,128)(2,1)} %bitcast.8, s32[1,512]{1,0:T(1,128)} %refs_3_.1, ...), custom_call_target="tpu_custom_call" | custom-call | tf_op jit(solution)/shard_map/pallas_call | solution.py:936
  96.3 5.3 %shard_map.358 = (f32[128,768]{1,0:T(8,128)}, f32[128,768]{1,0:T(8,128)}, f32[256,768]{1,0:T(8,128)}, f32[96,768]{1,0:T(8,128)}, f32[96,768]{1,0:T(8,128)}, /*in...) custom-call(f32[128,768]{1,0:T(8,128)} %get-tuple-element.43.layer, ...), custom_call_target="tpu_custom_call" | custom-call | tf_op jit(solution)/shard_map/pallas_call | solution.py:1010
